TPU v7x, 32 devices: a whole 2x2x4 slice. The times are simulated.
32 devices in a mesh: ka: 16 (over z, x, core), band: 2 (over y).
Axes of the slice: x: 2, y: 2, z: 4, core: 2. Of those that a mesh axis runs over, the one named last changes fastest.
Arguments:
- valence_orbitals: bfloat16 [16, 32, 64, 64, 128], P('ka', None, None, 'band'), may hold values from -6 to 6
- conduction_orbitals: bfloat16 [16, 1, 64, 64, 128], P(None, None, 'ka', 'band'), may hold values from -6 to 6
- valence_energy: float32 [16, 32], P('ka'), may hold values from -1.5 to -0.1
- conduction_energy: float32 [16, 1], replicated, may hold values from 0.1 to 1.5
- valence_select: int32 [16, 16], P('ka'), may hold values from 0 to 31, as said below
- shifted_index: int32 [16], replicated, may hold values from 0 to 15, each once
- wave_vectors: int32 [3, 2048], replicated, may hold values from -16 to 15
- frequency: float32 [1], replicated, may hold values from 0.3 to 1
Outputs:
- chi_zero: float32 [2, 2048, 2048], P(None, ('ka', 'band'))
Inputs may be any that keep to these rules, and one draw needn't show every extreme that they name: `valence_select`: each row holds 16 different band numbers. `shifted_index`: every k point is the partner of exactly one k point.
All inputs are finite; a program needn't handle non-finite values.
Results may differ from a plain program's by a relative error of at most 0.025.
Values may be sent and summed in bfloat16 or wider, within the bound.
A program may use at most 320 MiB of HBM per device.

v0:
```python
import math

import jax
import jax.numpy as jnp
from jax import lax
from jax.sharding import PartitionSpec as P


def depth_matrix(grid_size):
    positions = jnp.arange(grid_size, dtype=jnp.int32)
    phase_index = positions[:, None] * positions[None, :] % grid_size
    angle_value = phase_index.astype(jnp.float32) * (2.0 * math.pi / grid_size)
    cosine = jnp.cos(angle_value)
    sine_part = jnp.sin(angle_value)
    upper_half = jnp.concatenate([cosine, -sine_part], axis=1)
    lower_half = jnp.concatenate([sine_part, cosine], axis=1)
    return jnp.concatenate([upper_half, lower_half], axis=0).astype(jnp.bfloat16)


def column_matrix(grid_size):
    positions = jnp.arange(grid_size, dtype=jnp.int32)
    phase_index = positions[:, None] * positions[None, :] % grid_size
    angle_value = phase_index.astype(jnp.float32) * (2.0 * math.pi / grid_size)
    return jnp.concatenate([jnp.cos(angle_value), jnp.sin(angle_value)], axis=0).astype(
        jnp.bfloat16
    )


def shards(
    valence_orbitals,
    conduction_orbitals,
    valence_energy,
    conduction_energy,
    valence_select,
    shifted_index,
    wave_vectors,
    frequency,
):
    grid_size = valence_orbitals.shape[2]
    slab_width = valence_orbitals.shape[3]
    kpoint_count = lax.axis_size("ka")
    band_count = lax.axis_size("band")
    kpoint_rank = lax.axis_index("ka")
    band_rank = lax.axis_index("band")
    vector_count = wave_vectors.shape[1]
    block_rows = vector_count // (kpoint_count * band_count)
    permuted = (
        wave_vectors.reshape(3, kpoint_count, band_count, block_rows)
        .transpose(0, 2, 1, 3)
        .reshape(3, vector_count)
    )
    wrapped = jnp.mod(permuted, grid_size)
    twice = 2 * grid_size
    first_index = wrapped[1] * twice + wrapped[2]
    second_index = (grid_size + wrapped[1]) * twice + grid_size + wrapped[2]
    third_index = wrapped[1] * twice + grid_size + wrapped[2]
    fourth_index = (grid_size + wrapped[1]) * twice + wrapped[2]
    plane_coord = band_rank * slab_width + jnp.arange(slab_width, dtype=jnp.int32)
    plane_phase = wrapped[0][None, :] * plane_coord[:, None] % grid_size
    plane_angle = plane_phase.astype(jnp.float32) * (2.0 * math.pi / grid_size)
    norm_scale = float(grid_size) ** (-1.5)
    plane_cos = jnp.cos(plane_angle) * norm_scale
    plane_sin = jnp.sin(plane_angle) * norm_scale
    depth_table = depth_matrix(grid_size)
    column_table = column_matrix(grid_size)
    selected = jnp.take(valence_orbitals[0], valence_select[0], axis=0)
    selected_count = selected.shape[0]
    val_energies = jnp.take(valence_energy[0], valence_select[0])
    partner = shifted_index[kpoint_rank]
    cond_energies = lax.dynamic_index_in_dim(conduction_energy, partner, 0, keepdims=False)
    energy_gap = val_energies[None, :] - cond_energies[:, None]
    weight = (
        2.0
        * energy_gap
        / (energy_gap * energy_gap + frequency[0] * frequency[0])
        / (kpoint_count * selected_count)
    )

    def item_terms(columns):
        cond_real = columns[..., :grid_size].astype(jnp.float32)
        cond_imag = columns[..., grid_size:].astype(jnp.float32)
        val_real = selected[..., :grid_size].astype(jnp.float32)
        val_imag = selected[..., grid_size:].astype(jnp.float32)
        pair_values = jnp.concatenate(
            [
                val_real * cond_real[None] + val_imag * cond_imag[None],
                val_real * cond_imag[None] - val_imag * cond_real[None],
            ],
            axis=-1,
        ).astype(jnp.bfloat16)
        spectrum = jnp.dot(
            pair_values.reshape(-1, twice), depth_table, preferred_element_type=jnp.float32
        )
        spectrum = spectrum.astype(jnp.bfloat16).reshape(pair_values.shape)
        mixed_part = jnp.einsum(
            "ky,nyxc->nxkc", column_table, spectrum, preferred_element_type=jnp.float32
        )
        flat_view = mixed_part.reshape(selected_count, slab_width, twice * twice)
        real_cols = jnp.take(flat_view, first_index, axis=2) + jnp.take(
            flat_view, second_index, axis=2
        )
        imag_cols = jnp.take(flat_view, third_index, axis=2) - jnp.take(
            flat_view, fourth_index, axis=2
        )
        density_real = jnp.sum(plane_cos[None] * real_cols + plane_sin[None] * imag_cols, axis=1)
        density_imag = jnp.sum(plane_cos[None] * imag_cols - plane_sin[None] * real_cols, axis=1)
        return jnp.stack([density_real, density_imag])

    reordered = jnp.take(conduction_orbitals, shifted_index, axis=0)
    partial_value = lax.map(
        item_terms, lax.all_to_all(reordered, "ka", split_axis=0, concat_axis=2, tiled=True)[0]
    )
    shared = lax.psum_scatter(
        partial_value.astype(jnp.bfloat16), "band", scatter_dimension=3, tiled=True
    )
    density = lax.all_gather(shared, "band", axis=3, tiled=True)
    weighted = (weight[:, None, :, None] * shared.astype(jnp.float32)).astype(jnp.bfloat16)
    contract_dims = (((0, 1, 2), (0, 1, 2)), ((), ()))
    swapped = jnp.stack([weighted[:, 1], -weighted[:, 0]], axis=1)
    real_rows = lax.dot_general(
        weighted, density, contract_dims, preferred_element_type=jnp.float32
    )
    imag_rows = lax.dot_general(swapped, density, contract_dims, preferred_element_type=jnp.float32)
    chi_block = lax.psum_scatter(
        jnp.stack([real_rows, imag_rows], axis=1).astype(jnp.bfloat16),
        "ka",
        scatter_dimension=0,
        tiled=True,
    ).astype(jnp.float32)
    chi_block = chi_block.reshape(block_rows, 2, band_count, kpoint_count, block_rows).transpose(
        0, 1, 3, 2, 4
    )
    chi_block = chi_block.reshape(block_rows, 2, vector_count)
    return chi_block.transpose(1, 0, 2)


def solution(mesh):
    in_specs = (
        P("ka", None, None, "band", None),
        P(None, None, "ka", "band", None),
        P("ka", None),
        P(),
        P("ka", None),
        P(),
        P(),
        P(),
    )
    out_specs = P(None, ("ka", "band"), None)
    return jax.shard_map(shards, mesh=mesh, in_specs=in_specs, out_specs=out_specs, check_vma=False)
```

profile of v0, /device:TPU:0, one launch (start us, length us, event | category | flops | bytes accessed | tf_op | source)
XLA Modules:
  0.0 532.5 jit_solution(12039841463085187021)
XLA Ops:
  9.5 7.4 %all-to-all-start = ((bf16[16,1,4,32,128]{4,3,2,1,0:T(8,128)(2,1)}), bf16[16,1,4,32,128]{4,3,2,1,0:T(8,128)(2,1)S(1)}, u32[]{:S(2)}, u32[]{:S(2)}) async-start(bf16[16,1,4,32,128]{4,3,2,1,0:T(8,128)(2,1)} %bitcast_select_fusion), calls=%async_computation | async-start | bytes 1048576 | tf_op jit(solution)/shard_map/all_to_all | solution.py:111
  20.8 1.3 copy.30
  22.1 1.3 copy.35
  23.4 10.7 %gather_fusion.1 = bf16[16,64,32,128]{3,2,1,0:T(8,128)(2,1)} fusion(bf16[32,64,32,128]{3,2,1,0:T(8,128)(2,1)} %bitcast.107, s32[1024]{0:T(1024)S(1)} %pad_clamp_fusion.1), kind=kCustom, calls=%fused_computation.5 | custom fusion | bytes 16777280 | tf_op jit(solution)/shard_map/jit(_take)/gather | solution.py:66
  34.1 7.5 %broadcast_select_fusion = bf16[16,64,32,128]{3,2,1,0:T(8,128)(2,1)} fusion(bf16[16,64,32,128]{3,2,1,0:T(8,128)(2,1)} %gather_fusion.1, pred[16]{0:T(512)(128)(4,1)S(1)} %compare_and_fusion.5), kind=kLoop, calls=%fused_computation.28 | loop fusion | flops 4194304 | bytes 16777232 | tf_op jit(solution)/shard_map/jit(_take)/select_n | solution.py:66
  41.9 12.4 %fusion.1 = (bf16[16,64,32,64]{3,2,1,0:T(8,128)(2,1)S(1)}, bf16[16,64,32,64]{3,2,1,0:T(8,128)(2,1)}) fusion(f32[64,32,64]{2,1,0:T(8,128)S(1)} %get-tuple-element.33, f32[64,32,64]{2,1,0:T(8,128)S(1)} %get-tuple-element.32, bf16[16,64,32,128]{3,2,1,0:T(8,128)(2,1)} %broadcast_select_fusion), kind=kLoop, calls=%fused_computation.13 | loop fusion | flops 20971520 | bytes 17825792 | tf_op jit(solution)/shard_map/convert.23
  54.3 7.3 %convolution_convert_fusion = bf16[32768,128]{1,0:T(8,128)(2,1)S(1)} fusion(bf16[32768,64]{1,0:T(8,128)(2,1)} %bitcast.104, bf16[32768,64]{1,0:T(8,128)(2,1)S(1)} %bitcast.103, bf16[64,64]{0,1:T(8,128)(2,1)S(1)} %get-tuple-element.69, bf16[64,64]{0,1:T(8,128)(2,1)S(1)} %fusion.35, bf16[64,64]{0,1:T(8,128)(2,1)S(1)} %get-tuple-element.68), kind=kOutput, calls=%fused_computation.7 | convolution fusion | flops 1094844416 | bytes 16801792 | tf_op jit(solution)/shard_map/while/body/eval_jaxpr/dot_general | solution.py:91
  61.7 13.3 %convolution_bitcast_fusion = f32[16,32,128,128]{2,3,1,0:T(8,128)} fusion(bf16[16,64,32,128]{3,2,1,0:T(8,128)(2,1)S(1)} %bitcast.102, bf16[64,64]{0,1:T(8,128)(2,1)S(1)} %fusion.35, bf16[64,64]{0,1:T(8,128)(2,1)S(1)} %get-tuple-element.69), kind=kOutput, calls=%fused_computation.20 | convolution fusion | flops 1073774592 | bytes 41959424 | tf_op jit(solution)/shard_map/while/body/eval_jaxpr/ky,nyxc->nxkc/dot_general | solution.py:95
  74.9 98.4 %copy.42 = f32[16,32,128,128]{1,0,3,2:T(8,128)} copy(f32[16,32,128,128]{2,3,1,0:T(8,128)} %convolution_bitcast_fusion) | data formatting | bytes 67108864 | tf_op jit(solution)/shard_map/while/body/eval_jaxpr/reshape | solution.py:98
  173.3 39.5 %gather_fusion.6 = f32[2048,16,32]{2,1,0:T(8,128)} fusion(f32[16,32,16384]{1,0,2:T(8,128)} %bitcast.40, s32[2048]{0:T(1024)S(1)} %get-tuple-element.67), kind=kCustom, calls=%fused_computation.3.clone | custom fusion | bytes 8396800 | tf_op jit(solution)/shard_map/while/body/eval_jaxpr/jit(_take)/gather | solution.py:102
  212.9 39.6 %gather_fusion.3 = f32[2048,16,32]{2,1,0:T(8,128)} fusion(f32[16,32,16384]{1,0,2:T(8,128)} %bitcast.40, s32[2048]{0:T(1024)S(1)} %get-tuple-element.57), kind=kCustom, calls=%fused_computation.clone | custom fusion | bytes 8396800 | tf_op jit(solution)/shard_map/while/body/eval_jaxpr/jit(_take)/gather | solution.py:99
  252.4 39.5 %gather_fusion.5 = f32[2048,16,32]{2,1,0:T(8,128)} fusion(f32[16,32,16384]{1,0,2:T(8,128)} %bitcast.40, s32[2048]{0:T(1024)S(1)} %get-tuple-element.56), kind=kCustom, calls=%fused_computation.2.clone | custom fusion | bytes 8396800 | tf_op jit(solution)/shard_map/while/body/eval_jaxpr/jit(_take)/gather | solution.py:102
  291.9 39.6 %gather_fusion.4 = f32[2048,16,32]{2,1,0:T(8,128)} fusion(f32[16,32,16384]{1,0,2:T(8,128)} %bitcast.40, s32[2048]{0:T(1024)S(1)} %get-tuple-element.66), kind=kCustom, calls=%fused_computation.1.clone | custom fusion | bytes 8396800 | tf_op jit(solution)/shard_map/while/body/eval_jaxpr/jit(_take)/gather | solution.py:99
  331.5 50.3 %add_reduce_fusion = (bf16[16,2048]{0,1:T(8,128)(2,1)S(1)}, bf16[16,2048]{0,1:T(8,128)(2,1)}) fusion(f32[32,2048]{0,1:T(8,128)S(1)} %copy-done.4, f32[32,2048]{0,1:T(8,128)S(1)} %copy-done.3, f32[2048,16,32]{2,1,0:T(8,128)} %gather_fusion.4, pred[2048]{0:T(1024)(128)(4,1)S(1)} %get-tuple-element.64, f32[2048,16,32]{2,1,0:T(8,128)} %gather_fusion.3, ...), kind=kLoop, calls=%fused_computation.19 | loop fusion | flops 14614528 | bytes 17440768 | tf_op jit(solution)/shard_map/while/body/eval_jaxpr/reduce_sum | solution.py:105
  381.8 1.2 copy.39
  389.4 6.2 %reduce-scatter.3.cloned.1.call-done = bf16[1,2,16,1024]{3,2,1,0:T(8,128)(2,1)} async-done(((bf16[1,2,16,2048]{3,2,1,0:T(8,128)(2,1)}), bf16[1,2,16,1024]{3,2,1,0:T(8,128)(2,1)}) %reduce-scatter.3.cloned.1.call-update) | async-done | bytes 65552 | tf_op jit(solution)/shard_map/reduce_scatter | solution.py:113
  396.6 5.2 all_gather.3
  401.7 1.3 fusion.8
  403.0 3.2 fusion.9
  406.3 6.2 %pad_maximum_fusion = bf16[1024,2,2048]{2,0,1:T(8,128)(2,1)} fusion(bf16[1024,1,2048]{2,0,1:T(8,128)(2,1)} %fusion.9, bf16[1024,1,2048]{2,0,1:T(8,128)(2,1)S(1)} %fusion.8), kind=kLoop, calls=%fused_computation.24 | loop fusion | flops 4194304 | bytes 16777216 | tf_op jit(solution)/shard_map/stack | solution.py:125
  412.5 104.8 %reduce-scatter.5.cloned.1.call-done = bf16[64,2,2048]{2,0,1:T(8,128)(2,1)} async-done(((bf16[1024,2,2048]{2,0,1:T(8,128)(2,1)}), bf16[64,2,2048]{2,0,1:T(8,128)(2,1)}) %reduce-scatter.5.cloned.1.call-update) | async-done | bytes 524304 | tf_op jit(solution)/shard_map/reduce_scatter | solution.py:124
  517.2 1.9 reshape.241
  519.2 2.4 copy.40
  521.6 4.1 reshape.240
  (49 shorter events, 11.7 us)
Async XLA Ops:
  6.5 1.4 copy-start
  9.5 32.1 %all-to-all-start = ((bf16[16,1,4,32,128]{4,3,2,1,0:T(8,128)(2,1)}), bf16[16,1,4,32,128]{4,3,2,1,0:T(8,128)(2,1)S(1)}, u32[]{:S(2)}, u32[]{:S(2)}) async-start(bf16[16,1,4,32,128]{4,3,2,1,0:T(8,128)(2,1)} %bitcast_select_fusion), calls=%async_computation | async-start | bytes 1048576 | tf_op jit(solution)/shard_map/all_to_all | solution.py:111
  16.9 378.8 %reduce-scatter.3.cloned.1.call-start = ((), (), s32[]{:S(2)}) async-start(), calls=%async_computation.3 | async-start | bytes 196608 | tf_op jit(solution)/shard_map/reduce_scatter | solution.py:113
  173.3 158.2 %copy-start.3 = (f32[32,2048]{0,1:T(8,128)S(1)}, f32[32,2048]{0,1:T(8,128)}, u32[]{:S(2)}) copy-start(f32[32,2048]{0,1:T(8,128)} %copy.30) | copy-start | bytes 786436
  173.3 158.2 %copy-start.4 = (f32[32,2048]{0,1:T(8,128)S(1)}, f32[32,2048]{0,1:T(8,128)}, u32[]{:S(2)}) copy-start(f32[32,2048]{0,1:T(8,128)} %copy.35) | copy-start | bytes 786436
  331.5 52.5 %copy-start.6 = (s32[16]{0:T(128)S(1)}, s32[16]{0:T(128)}, u32[]{:S(2)}) copy-start(s32[16]{0:T(128)} %param.15) | copy-start | bytes 196
  331.5 54.5 %copy-start.2 = (f32[1,32]{1,0:T(1,128)S(1)}, f32[1,32]{1,0:T(1,128)}, u32[]{:S(2)}) copy-start(f32[1,32]{1,0:T(1,128)} %param.12) | copy-start | bytes 388
  331.5 56.5 %copy-start.7 = (f32[16,1]{0,1:T(1,128)S(1)}, f32[16,1]{0,1:T(1,128)}, u32[]{:S(2)}) copy-start(f32[16,1]{0,1:T(1,128)} %param.13) | copy-start | bytes 196
  331.5 57.2 %copy-start.5 = (s32[1,16]{1,0:T(1,128)S(1)}, s32[1,16]{1,0:T(1,128)}, u32[]{:S(2)}) copy-start(s32[1,16]{1,0:T(1,128)} %param.14) | copy-start | bytes 196
  383.9 133.3 %reduce-scatter.5.cloned.1.call-start = ((), (), s32[]{:S(2)}) async-start(), calls=%async_computation.4 | async-start | bytes 8912896 | tf_op jit(solution)/shard_map/reduce_scatter | solution.py:124
  403.0 122.7 %copy-start.1 = (bf16[16,1,4,32,128]{4,3,2,1,0:T(8,128)(2,1)S(1)}, bf16[16,1,4,32,128]{4,3,2,1,0:T(8,128)(2,1)}, u32[]{:S(2)}) copy-start(bf16[16,1,4,32,128]{4,3,2,1,0:T(8,128)(2,1)} %param.11) | copy-start | bytes 1572868
Sparse Core Ops, SparseCore 0:
  384.0 11.5 reduce-scatter.2
  412.6 104.5 reduce-scatter.4
where the time goes:
time: 537 us; the launch traced here: 533 us
  local copies, waits for them, and re-layouts  283 us (53%)
  waiting for transfers between devices  111 us (21%)
  other arithmetic  84.1 us (16%)
  matrix products  25.1 us (5%)
  between operations  16.4 us (3%)
  starting transfers between devices  7.44 us (1%)
    reduce_scatter x1, waiting for transfers between devices, shards(): lax.psum_scatter(jnp.stack([real_rows, imag_rows], axis=1).astype(jnp.bfl...  105 us
    reshape x1, local copies, waits for them, and re-layouts, item_terms(): flat_view = mixed_part.reshape(selected_count, slab_width, twice * twice)  98.4 us
    reduce_sum x1, other arithmetic, item_terms(): jnp.sum(plane_cos[None] * real_cols + plane_sin[None] * imag_cols, axis=1)  50.3 us
    gather x1, local copies, waits for them, and re-layouts, item_terms(): jnp.take(flat_view, second_index, axis=2)  39.6 us
    gather x1, local copies, waits for them, and re-layouts, item_terms(): jnp.take(flat_view, first_index, axis=2)  39.6 us
    gather x1, local copies, waits for them, and re-layouts, item_terms(): jnp.take(flat_view, fourth_index, axis=2)  39.5 us
    gather x1, local copies, waits for them, and re-layouts, item_terms(): jnp.take(flat_view, third_index, axis=2)  39.5 us
    dot_general x1, matrix products, item_terms(): jnp.einsum('ky,nyxc->nxkc', column_table, spectrum, preferred_element_typ...  13.3 us
  transfers between devices with their start and end apart: 3, of which 2 were waited for; matrix products, arithmetic and copies ran while one was open for 5% of the time, Pallas kernels for 0%

commit v1 on v0

v1 whole, which is shorter than its diff:
```python
import functools
import math

import jax
import jax.numpy as jnp
import numpy as np
from jax import lax
from jax.experimental import pallas as pl
from jax.experimental.pallas import tpu as pltpu
from jax.sharding import PartitionSpec as P

SUB = 8
GROUP = 4


def column_tables(grid):
    half = grid // 2
    count = grid // 4
    y = np.arange(half)
    eye = np.eye(SUB)
    tables = []
    for parity in (0, 1):
        wave = 2 * np.arange(count) - count + parity
        angle = 2.0 * np.pi * ((wave[:, None] * y[None, :]) % grid) / grid
        both = np.stack([np.cos(angle), np.sin(angle)], axis=1).reshape(2 * count, half)
        tables.append(np.kron(both, eye))
    return np.stack(tables)


def depth_table(grid):
    half = grid // 2
    wave = np.arange(half) - half // 2
    angle = 2.0 * np.pi * ((np.arange(grid)[:, None] * wave[None, :]) % grid) / grid
    cosine, sine = np.cos(angle), np.sin(angle)
    real = np.concatenate([cosine, sine, -sine, cosine])
    imag = np.concatenate([-sine, cosine, -cosine, -sine])
    out = np.zeros((GROUP, 4 * grid, 2, GROUP, half))
    for j in range(GROUP):
        out[j, :, 0, j, :] = real
        out[j, :, 1, j, :] = imag
    return out.reshape(GROUP * 4 * grid, 2 * GROUP * half)


def phase_table(grid, slab):
    half = grid // 2
    wave = np.arange(half) - half // 2
    angle = 2.0 * np.pi * ((np.arange(grid)[:, None] * wave[None, :]) % grid) / grid
    parts = []
    for value in (np.cos(angle), np.sin(angle)):
        value = value * float(grid) ** (-1.5)
        high = value.astype(jnp.bfloat16).astype(np.float64)
        parts += [high, value - high]
    stacked = np.stack([part.reshape(grid // slab, slab, half) for part in parts], axis=1)
    return stacked.reshape(grid // slab, 4 * slab, half)


def density_kernel(
    select_ref,
    where_ref,
    vener_ref,
    cener_ref,
    freq_ref,
    v_ref,
    c_ref,
    waves_ref,
    col_ref,
    depth_ref,
    phase_ref,
    out_ref,
    cr_ref,
    ci_ref,
    hot_ref,
    mid_ref,
    rows_ref,
    cs_ref,
):
    step = pl.program_id(0)
    bands = pl.num_programs(0)
    grid, slab, twice = c_ref.shape
    half = grid // 2
    count = grid // 4
    width = min(2 * SUB, slab)
    blocks = width // SUB
    vectors = waves_ref.shape[1]

    @pl.when(step == 0)
    def _():
        values = c_ref[...].astype(jnp.float32)
        turned = pltpu.roll(values.reshape(grid * slab, twice), grid, 1).reshape(values.shape)
        low = lax.broadcasted_iota(jnp.int32, values.shape, 2) < grid
        cr_ref[...] = jnp.where(low, values, -turned)
        ci_ref[...] = jnp.where(low, turned, values)
        gy = waves_ref[1:2, :] + count
        parity = gy % 2
        key = ((parity * count + (gy - parity) // 2) * half) + waves_ref[2:3, :] + count
        iota = lax.broadcasted_iota(jnp.int32, (half, vectors), 0)
        for q in range(half):
            hot_ref[q * half : (q + 1) * half, :] = jnp.where(
                iota == key - q * half, 1.0, 0.0
            ).astype(jnp.bfloat16)
        hot_x = jnp.where(iota == waves_ref[0:1, :] + count, 1.0, 0.0).astype(jnp.bfloat16)
        table = jnp.dot(phase_ref[0], hot_x, preferred_element_type=jnp.float32)
        cs_ref[0] = table[:slab] + table[slab : 2 * slab]
        cs_ref[1] = table[2 * slab : 3 * slab] + table[3 * slab :]

    for start in range(0, slab, width):
        span = slice(start, start + width)
        v = v_ref[0, 0, :, span, :].astype(jnp.float32)
        swap = (v * ci_ref[:, span, :]).reshape(grid * width, twice)
        pair = v * cr_ref[:, span, :] + pltpu.roll(swap, grid, 1).reshape(v.shape)
        top, bottom = pair[:half], pair[half:]
        for parity, mixed in ((0, top + bottom), (1, top - bottom)):
            data = jnp.concatenate(
                [
                    mixed[:, b * SUB : (b + 1) * SUB, :].reshape(half * SUB, twice)
                    for b in range(blocks)
                ],
                axis=1,
            ).astype(jnp.bfloat16)
            got = jnp.dot(col_ref[parity], data, preferred_element_type=jnp.float32)
            for r in range(2 * count):
                piece = jnp.concatenate(
                    [
                        got[r * SUB : (r + 1) * SUB, b * twice : (b + 1) * twice]
                        for b in range(blocks)
                    ],
                    axis=0,
                )
                lane = (parity * 2 * count + r) * twice
                mid_ref[step, span, lane : lane + twice] = piece.astype(mid_ref.dtype)

    @pl.when(step == bands - 1)
    def _():
        total = mid_ref.shape[0] * slab
        depth = depth_ref.shape[0]
        piece = depth_ref.shape[1] // 2
        for g in range(half // GROUP):
            left = mid_ref[:, :, g * depth : (g + 1) * depth].reshape(total, depth)
            got = jnp.dot(
                left.astype(jnp.bfloat16), depth_ref[...], preferred_element_type=jnp.float32
            ).astype(jnp.bfloat16)
            rows_ref[:total, g * piece : (g + 1) * piece] = got[:, :piece]
            rows_ref[total:, g * piece : (g + 1) * piece] = got[:, piece:]

        nbands = mid_ref.shape[0]
        row = lax.broadcasted_iota(jnp.int32, (nbands, 128), 0)
        partner_energy = cener_ref[where_ref[0]]
        energy = jnp.zeros((nbands, 128), jnp.float32)
        for n in range(nbands):
            energy = jnp.where(row == n, vener_ref[select_ref[n]], energy)
        gap = energy - partner_energy
        freq = freq_ref[0]
        weight = 2.0 * gap / (gap * gap + freq * freq) / where_ref[2].astype(jnp.float32)
        scale = jnp.sqrt(-weight)[:, :1]
        tile = 256

        def chunk(i, carry):
            cols = pl.ds(pl.multiple_of(i * tile, tile), tile)
            got = jnp.dot(rows_ref[...], hot_ref[:, cols], preferred_element_type=jnp.float32)
            real = got[:total].reshape(nbands, slab, tile)
            imag = got[total:].reshape(nbands, slab, tile)
            cosine, sine = cs_ref[0, :, cols][None], cs_ref[1, :, cols][None]
            dens_real = jnp.sum(cosine * real + sine * imag, axis=1) * scale
            dens_imag = jnp.sum(cosine * imag - sine * real, axis=1) * scale
            out_ref[:nbands, cols] = dens_real.astype(out_ref.dtype)
            out_ref[nbands:, cols] = dens_imag.astype(out_ref.dtype)
            return carry

        lax.fori_loop(0, vectors // tile, chunk, 0)


def partial_density(valence, conduction, select, where, vener, cener, freq, waves):
    _, _, grid, slab, twice = valence.shape
    nbands = select.shape[0]
    vectors = waves.shape[1]
    half = grid // 2
    col = jnp.asarray(column_tables(grid), jnp.bfloat16)
    depth = jnp.asarray(depth_table(grid), jnp.bfloat16)
    phase = jnp.asarray(phase_table(grid, slab), jnp.bfloat16)
    mid_type = jnp.bfloat16 if slab >= 16 else jnp.float32
    return pl.pallas_call(
        density_kernel,
        out_shape=jax.ShapeDtypeStruct((2 * nbands, vectors), jnp.bfloat16),
        grid_spec=pltpu.PrefetchScalarGridSpec(
            num_scalar_prefetch=5,
            grid=(nbands,),
            in_specs=[
                pl.BlockSpec((1, 1, grid, slab, twice), lambda n, sel, *_: (0, sel[n], 0, 0, 0)),
                pl.BlockSpec(conduction.shape, lambda n, *_: (0, 0, 0)),
                pl.BlockSpec(waves.shape, lambda n, *_: (0, 0)),
                pl.BlockSpec(col.shape, lambda n, *_: (0, 0, 0)),
                pl.BlockSpec(depth.shape, lambda n, *_: (0, 0)),
                pl.BlockSpec((1,) + phase.shape[1:], lambda n, sel, at, *_: (at[1], 0, 0)),
            ],
            out_specs=pl.BlockSpec((2 * nbands, vectors), lambda n, *_: (0, 0)),
            scratch_shapes=[
                pltpu.VMEM((grid, slab, twice), jnp.float32),
                pltpu.VMEM((grid, slab, twice), jnp.float32),
                pltpu.VMEM((half * half, vectors), jnp.bfloat16),
                pltpu.VMEM((nbands, slab, 2 * half * twice), mid_type),
                pltpu.VMEM((2 * nbands * slab, half * half), jnp.bfloat16),
                pltpu.VMEM((2, slab, vectors), jnp.float32),
            ],
        ),
        compiler_params=pltpu.CompilerParams(
            dimension_semantics=("arbitrary",), vmem_limit_bytes=50 * 1024 * 1024
        ),
        cost_estimate=pl.CostEstimate(
            flops=20_000_000_000, bytes_accessed=12_000_000, transcendentals=0
        ),
    )(select, where, vener, cener, freq, valence, conduction, waves, col, depth, phase)


def shards(
    valence_orbitals,
    conduction_orbitals,
    valence_energy,
    conduction_energy,
    valence_select,
    shifted_index,
    wave_vectors,
    frequency,
):
    grid, slab, twice = valence_orbitals.shape[2:]
    kpoints, bands = lax.axis_size("ka"), lax.axis_size("band")
    ka, band = lax.axis_index("ka"), lax.axis_index("band")
    vectors = wave_vectors.shape[1]
    nocc = valence_select.shape[1]
    rows = vectors // (kpoints * bands)
    reordered = jnp.take(conduction_orbitals[:, 0], shifted_index, axis=0, mode="clip")
    conduction = lax.all_to_all(reordered, "ka", split_axis=0, concat_axis=0, tiled=True)
    conduction = conduction.reshape(grid, slab, twice)
    where = jnp.stack([shifted_index[ka], band, jnp.int32(kpoints * nocc)])
    part = partial_density(
        valence_orbitals,
        conduction,
        valence_select[0],
        where,
        valence_energy[0],
        conduction_energy[:, 0],
        frequency,
        wave_vectors,
    )
    shared = lax.psum_scatter(part, "band", scatter_dimension=1, tiled=True)
    full = lax.all_gather(shared, ("ka", "band"), axis=0, tiled=False)
    full = full.reshape(kpoints, bands, 2 * nocc, vectors // bands)
    full = full.transpose(0, 2, 1, 3).reshape(kpoints, 2 * nocc, vectors)
    left = lax.dynamic_slice_in_dim(full, (ka * bands + band) * rows, rows, axis=2)
    real, imag = left[:, :nocc], left[:, nocc:]
    left_real = jnp.concatenate([-real, -imag], axis=1)
    left_imag = jnp.concatenate([-imag, real], axis=1)
    sides = jnp.stack([left_real, left_imag], axis=0)
    return jnp.einsum("ckns,knt->cst", sides, full, preferred_element_type=jnp.float32)


def solution(mesh):
    in_specs = (
        P("ka", None, None, "band", None),
        P(None, None, "ka", "band", None),
        P("ka", None),
        P(),
        P("ka", None),
        P(),
        P(),
        P(),
    )
    out_specs = P(None, ("ka", "band"), None)
    return jax.shard_map(shards, mesh=mesh, in_specs=in_specs, out_specs=out_specs, check_vma=False)
```

time: 537 us -> 146 us (0.27)
  local copies, waits for them, and re-layouts: 283 us -> 12.4 us
  other arithmetic: 84.1 us -> 2.42 us
  waiting for transfers between devices: 111 us -> 82 us
  Pallas kernels: 0 us -> 25.4 us
  matrix products: 25.1 us -> 1.45 us
    gather x7 -> x1, local copies, waits for them, and re-layouts: 170 us -> 1.4 us  [shards(): jnp.take(conduction_orbitals[:, 0], shifted_index, axis=0, mode='clip')]
    reduce_scatter x2 -> x1, waiting for transfers between devices: 111 us -> 9.79 us  [shards(): shared = lax.psum_scatter(part, 'band', scatter_dimension=1, tiled=True)]
    reshape x4 -> x2, local copies, waits for them, and re-layouts: 99.3 us -> 6.61 us  [shards(): full = full.transpose(0, 2, 1, 3).reshape(kpoints, 2 * nocc, vectors)]
    all_gather x0 -> x1, waiting for transfers between devices: none -> 59.6 us  [shards(): full = lax.all_gather(shared, ('ka', 'band'), axis=0, tiled=False)]
    reduce_sum x1 -> x0, other arithmetic: 50.3 us -> none  [item_terms(): jnp.sum(plane_cos[None] * real_cols + plane_sin[None] * imag_cols, axis=1)]
    pallas_call x0 -> x1, Pallas kernels: none -> 25.4 us  [partial_density(): pl.pallas_call(density_kernel, out_shape=jax.ShapeDtypeStruct((2 * nbands...]
    dot_general x4 -> x1, matrix products: 25.1 us -> 1.45 us  [shards(): jnp.einsum('ckns,knt->cst', sides, full, preferred_element_type=jnp.float32)]
    another operation x5 -> x2, other arithmetic: 19.5 us -> 0.66 us  [the longest x1 0.62 us: shards(): where = jnp.stack([shifted_index[ka], band, jnp.int32(kpoints * nocc)])]
  transfers between devices with their start and end apart: 3 -> 3, of which waited for: 2 -> 3; matrix products, arithmetic and copies ran while one was open for 5% -> 1% of each run, Pallas kernels for 0% -> 0%
where the time goes in v1:
time: 146 us; the launch traced here: 145 us
  waiting for transfers between devices  82 us (56%)
  Pallas kernels  25.4 us (17%)
  between operations  14.2 us (10%)
  local copies, waits for them, and re-layouts  12.4 us (8%)
  starting transfers between devices  7.44 us (5%)
  other arithmetic  2.42 us (2%)
    all_gather x1, waiting for transfers between devices, shards(): full = lax.all_gather(shared, ('ka', 'band'), axis=0, tiled=False)  59.6 us
    pallas_call x1, Pallas kernels, partial_density(): pl.pallas_call(density_kernel, out_shape=jax.ShapeDtypeStruct((2 * nbands...  25.4 us
    all_to_all x1, waiting for transfers between devices, shards(): lax.all_to_all(reordered, 'ka', split_axis=0, concat_axis=0, tiled=True)  12.6 us
    reduce_scatter x1, waiting for transfers between devices, shards(): shared = lax.psum_scatter(part, 'band', scatter_dimension=1, tiled=True)  9.79 us
    all_to_all x1, starting transfers between devices, shards(): lax.all_to_all(reordered, 'ka', split_axis=0, concat_axis=0, tiled=True)  7.36 us
    reshape x2, local copies, waits for them, and re-layouts, shards(): full = full.transpose(0, 2, 1, 3).reshape(kpoints, 2 * nocc, vectors)  6.61 us
    transpose x1, local copies, waits for them, and re-layouts, shards(): full = full.transpose(0, 2, 1, 3).reshape(kpoints, 2 * nocc, vectors)  3.51 us
  transfers between devices with their start and end apart: 3, of which 3 were waited for; matrix products, arithmetic and copies ran while one was open for 1% of the time, Pallas kernels for 0%

profile of v1, /device:TPU:0, one launch (start us, length us, event | category | flops | bytes accessed | tf_op | source)
XLA Modules:
  0.0 145.3 jit_solution(587593764543217811)
XLA Ops:
  6.5 0.0 copy-start.2
  6.6 0.0 copy-start.3
  6.6 0.0 copy-start.4
  6.6 0.0 copy-start.1
  6.6 0.8 pad_clamp_fusion
  7.3 0.2 copy-done
  7.6 1.4 gather_fusion
  9.0 7.4 %all-to-all-start = ((bf16[16,4,32,128]{3,2,1,0:T(8,128)(2,1)}), bf16[16,4,32,128]{3,2,1,0:T(8,128)(2,1)S(1)}, u32[]{:S(2)}, u32[]{:S(2)}) async-start(bf16[16,4,32,128]{3,2,1,0:T(8,128)(2,1)} %gather_fusion), calls=%async_computation | async-start | bytes 1048576 | tf_op jit(solution)/shard_map/all_to_all | solution.py:231
  16.4 0.0 reduce-scatter.2.cloned.1.call-start
  16.4 0.0 copy-done.9
  16.4 0.6 dynamic_slice.6
  17.6 0.6 pad_add_fusion.where_ref
  18.3 12.6 %all-to-all-done = bf16[16,4,32,128]{3,2,1,0:T(8,128)(2,1)S(1)} async-done(((bf16[16,4,32,128]{3,2,1,0:T(8,128)(2,1)}), bf16[16,4,32,128]{3,2,1,0:T(8,128)(2,1)S(1)}, u32[]{:S(2)}, u32[]{:S(2)}) %all-to-all-start) | async-done | bytes 524320 | tf_op jit(solution)/shard_map/all_to_all | solution.py:231
  30.9 25.4 %shard_map.109 = bf16[32,2048]{1,0:T(8,128)(2,1)} custom-call(s32[16]{0:T(128)S(1)} %bitcast.21, s32[3]{0:T(128)S(1)} %pad_add_fusion.where_ref, f32[32]{0:T(128)S(1)} %bitcast.22, f32[16]{0:T(128)S(1)} %bitcast.23, f32[1]{0:T(128)S(6)} %copy.15.freq_ref, bf16[1,32,64,32,128]{4,3,2,1,0:T(8,128)(2,1)} %v_ref.1, bf16[64,32,128]{2,1,0:T(8,128)(2,1)S(1)} %bitcast.20, ...), custom_call_target="tpu_custom_call" | custom-call | flops 20000000000 | bytes 12000000 | tf_op jit(solution)/shard_map/pallas_call | solution.py:181
  56.3 0.0 reduce-scatter.2.cloned.1.call-update
  56.3 0.0 all-gather.3.cloned.1.call-start
  56.4 9.8 %reduce-scatter.2.cloned.1.call-done = bf16[32,1024]{1,0:T(8,128)(2,1)} async-done(((bf16[32,2048]{1,0:T(8,128)(2,1)}), bf16[32,1024]{1,0:T(8,128)(2,1)}) %reduce-scatter.2.cloned.1.call-update) | async-done | bytes 65552 | tf_op jit(solution)/shard_map/reduce_scatter | solution.py:244
  66.2 0.0 all-gather.3.cloned.1.call-update
  66.2 59.6 %all-gather.3.cloned.1.call-done = bf16[1024,1024]{1,0:T(8,128)(2,1)} async-done(((bf16[32,1024]{1,0:T(8,128)(2,1)}), bf16[1024,1024]{1,0:T(8,128)(2,1)}) %all-gather.3.cloned.1.call-update) | async-done | bytes 2097168 | tf_op jit(solution)/shard_map/all_gather | solution.py:245
  125.8 3.3 %copy.14 = bf16[16,2,4,8,1024]{4,3,1,2,0:T(8,128)(2,1)} copy(bf16[16,2,4,8,1024]{4,3,2,1,0:T(8,128)(2,1)} %bitcast.24) | data formatting | bytes 4194304 | tf_op jit(solution)/shard_map/reshape | solution.py:247
  129.2 3.5 %copy.12 = bf16[16,32,2,1024]{3,2,1,0:T(2,128)(2,1)} copy(bf16[16,32,2,1024]{3,1,2,0:T(8,128)(2,1)S(1)} %bitcast.25) | data formatting | bytes 4194304 | tf_op jit(solution)/shard_map/transpose | solution.py:247
  132.7 3.3 %reshape.23 = bf16[16,32,2048,1]{2,1,0,3:T(8,128)(2,1)S(1)} reshape(bf16[16,32,2,1024]{3,2,1,0:T(2,128)(2,1)} %copy.12) | data formatting | bytes 4194304 | tf_op jit(solution)/shard_map/reshape | solution.py:247
  136.0 1.0 fusion.4
  137.0 1.5 %convolution_bitcast_fusion = f32[2,64,2048]{2,1,0:T(8,128)} fusion(bf16[16,32,2048,1]{2,1,0,3:T(8,128)(2,1)S(1)} %reshape.23, bf16[1,16,32,64]{3,2,1,0:T(8,128)(2,1)S(1)} %get-tuple-element.9, bf16[1,16,32,64]{3,2,1,0:T(8,128)(2,1)S(1)} %get-tuple-element.8), kind=kOutput, calls=%fused_computation.1 | convolution fusion | flops 268500992 | bytes 3276800 | tf_op jit(solution)/shard_map/ckns,knt->cst/dot_general | solution.py:253
  (15 shorter events, 0.1 us)
Async XLA Ops:
  6.5 1.1 copy-start
  6.5 24.3 %copy-start.6 = (bf16[2,256,256]{2,1,0:T(8,128)(2,1)S(1)}, bf16[2,256,256]{2,1,0:T(8,128)(2,1)}, u32[]{:S(2)}) copy-start(bf16[2,256,256]{2,1,0:T(8,128)(2,1)} %constant.26.clone.col_ref) | copy-start | bytes 786436
  6.5 24.3 %copy-start.5 = (bf16[1024,256]{1,0:T(8,128)(2,1)S(1)}, bf16[1024,256]{1,0:T(8,128)(2,1)}, u32[]{:S(2)}) copy-start(bf16[1024,256]{1,0:T(8,128)(2,1)} %constant.27.clone.depth_ref) | copy-start | bytes 1572868
  6.5 24.3 %copy-start.7 = (bf16[2,128,32]{2,1,0:T(8,128)(2,1)S(1)}, bf16[2,128,32]{2,1,0:T(8,128)(2,1)}, u32[]{:S(2)}) copy-start(bf16[2,128,32]{2,1,0:T(8,128)(2,1)} %constant.28.clone.phase_ref) | copy-start | bytes 49156
  6.5 9.9 %copy-start.9 = (s32[16]{0:T(128)S(1)}, s32[16]{0:T(128)}, u32[]{:S(2)}) copy-start(s32[16]{0:T(128)} %param.16) | copy-start | bytes 196
  6.5 24.3 %copy-start.2 = (s32[1,16]{1,0:T(1,128)S(1)}, s32[1,16]{1,0:T(1,128)}, u32[]{:S(2)}) copy-start(s32[1,16]{1,0:T(1,128)} %param.15) | copy-start | bytes 196
  6.6 24.3 %copy-start.3 = (f32[1,32]{1,0:T(1,128)S(1)}, f32[1,32]{1,0:T(1,128)}, u32[]{:S(2)}) copy-start(f32[1,32]{1,0:T(1,128)} %param.13) | copy-start | bytes 388
  6.6 24.3 %copy-start.4 = (f32[16,1]{0,1:T(1,128)S(1)}, f32[16,1]{0,1:T(1,128)}, u32[]{:S(2)}) copy-start(f32[16,1]{0,1:T(1,128)} %param.14) | copy-start | bytes 196
  6.6 24.3 %copy-start.1 = (s32[3,2048]{1,0:T(4,128)S(1)}, s32[3,2048]{1,0:T(4,128)}, u32[]{:S(2)}) copy-start(s32[3,2048]{1,0:T(4,128)} %waves_ref.1) | copy-start | bytes 73732
  9.0 21.8 %all-to-all-start = ((bf16[16,4,32,128]{3,2,1,0:T(8,128)(2,1)}), bf16[16,4,32,128]{3,2,1,0:T(8,128)(2,1)S(1)}, u32[]{:S(2)}, u32[]{:S(2)}) async-start(bf16[16,4,32,128]{3,2,1,0:T(8,128)(2,1)} %gather_fusion), calls=%async_computation | async-start | bytes 1048576 | tf_op jit(solution)/shard_map/all_to_all | solution.py:231
  16.4 49.8 %reduce-scatter.2.cloned.1.call-start = ((), (), s32[]{:S(2)}) async-start(), calls=%async_computation.2 | async-start | bytes 196608 | tf_op jit(solution)/shard_map/reduce_scatter | solution.py:244
  56.3 69.5 %all-gather.3.cloned.1.call-start = ((), (), s32[]{:S(2)}) async-start(), calls=%async_computation.3 | async-start | bytes 2162688 | tf_op jit(solution)/shard_map/all_gather | solution.py:245
  125.8 3.3 %copy-start.8 = (bf16[1024,1024]{1,0:T(8,128)(2,1)S(1)}, bf16[1024,1024]{1,0:T(8,128)(2,1)}, u32[]{:S(2)}) copy-start(bf16[1024,1024]{1,0:T(8,128)(2,1)} %all-gather.3.cloned.1.call-done) | copy-start | bytes 6291460
Sparse Core Ops, SparseCore 0:
  56.5 9.6 reduce-scatter.1
  69.3 56.4 all-gather.2
